TPU v7x, 32 devices: a whole 2x2x4 slice. The times are simulated.
32 devices in a mesh: groups: 2 (over y), dp: 4 (over x, core), mp: 4 (over z).
Axes of the slice: x: 2, y: 2, z: 4, core: 2. Of those that a mesh axis runs over, the one named last changes fastest.
Arguments:
- tokens: int32 [16, 512], P(('groups', 'dp')), parts along dimension 0, may hold values from 0 to 128255
- acts: bfloat16 [8192, 20480], P(('groups', 'dp'), 'mp'), parts along dimension 0, may hold values from -6 to 6
- resid: bfloat16 [8192, 8192], P(('groups', 'dp'), 'mp'), parts along dimension 0, may hold values from -6 to 6
- cotangent: bfloat16 [8192, 8192], P(('groups', 'dp'), 'mp'), parts along dimension 0, may hold values from -6 to 6
- weight: bfloat16 [20480, 8192], P('mp'), may hold values from -0.0625 to 0.0625
- gain: bfloat16 [8192], P('mp'), may hold values from 0.099609375 to 1.8984375
- proj_in: bfloat16 [20480, 64], P('mp'), may hold values from -0.0390625 to 0.0390625
- proj_out: bfloat16 [8192, 64], P('mp'), may hold values from -0.0625 to 0.0625
- tok_weight: float32 [128256], replicated, may hold values from 0.25 to 4
- lengths: int32 [16], P(('groups', 'dp')), parts along dimension 0, may hold values from 128 to 512, as said below
- queries: bfloat16 [4096, 4096], P('dp', 'mp'), may hold values from -0.0234375 to 0.0234375
- query_ids: int32 [4096], replicated, may hold values from 0 to 255
Outputs:
- stream: bfloat16 [8192, 8192], P(('groups', 'dp'), 'mp'), parts along dimension 0
- scores: float32 [16, 256], P(('groups', 'dp')), parts along dimension 0
There are 2 independent parts, one for each index of `groups`. A program takes and returns all parts, laid end to end along the dimension named above; an argument that names none is the same for every part. Nothing has to cross between parts.
Inputs may be any that keep to these rules, and one draw needn't show every extreme that they name: `lengths`: document 0 has length 512.
All inputs are finite; a program needn't handle non-finite values.
Results may differ from a plain program's by a relative error of at most 0.015.
Values may be sent and summed in bfloat16 or wider, within the bound.
A program may use at most 320 MiB of HBM per device.

v0:
```python
import jax
import jax.numpy as jnp
from jax import lax
from jax.sharding import PartitionSpec as P

QG = 256


norm_eps = 1e-05


def norm_grad(pre_norm, scaled_cot, mean_sq, mean_cross):
    rstd = lax.rsqrt(mean_sq + norm_eps)
    return (rstd * (scaled_cot - pre_norm * rstd * rstd * mean_cross)).astype(jnp.bfloat16)


def group_table(own_ids, group_count):
    return (own_ids[:, None] == jnp.arange(group_count, dtype=jnp.int32)[None, :]).astype(
        jnp.float32
    )


def per_device(
    tokens,
    acts,
    resid,
    cotangent,
    weight,
    gain,
    proj_in,
    proj_out,
    tok_weight,
    lengths,
    queries,
    query_ids,
):
    doc_count = tokens.shape[0]
    seq_len = tokens.shape[1]
    tok_count = acts.shape[0]
    model_ways = lax.axis_size("mp")
    sketch_rank = proj_in.shape[1]
    feat_count = queries.shape[1]
    width_full = resid.shape[1] * model_ways
    partial_out = jnp.dot(acts, weight, preferred_element_type=jnp.float32)
    in_partial = jnp.dot(acts, proj_in, preferred_element_type=jnp.float32)
    alive_mask = jnp.arange(seq_len, dtype=jnp.int32)[None, :] < lengths[:, None]
    tok_scale = jnp.where(alive_mask, tok_weight[tokens], jnp.float32(0.0)) / jnp.sqrt(
        jnp.float32(seq_len)
    )
    tok_scale = tok_scale.reshape(tok_count)
    layer_out = lax.psum_scatter(
        partial_out.astype(jnp.bfloat16), "mp", scatter_dimension=1, tiled=True
    ).astype(jnp.float32)
    pre_norm = resid.astype(jnp.float32) + layer_out
    scaled_cot = gain.astype(jnp.float32)[None, :] * cotangent.astype(jnp.float32)
    row_sums = lax.psum(
        (jnp.sum(pre_norm * pre_norm, axis=1), jnp.sum(pre_norm * scaled_cot, axis=1)), "mp"
    )
    out_grad = norm_grad(
        pre_norm, scaled_cot, row_sums[0][:, None] / width_full, row_sums[1][:, None] / width_full
    )
    out_partial = jnp.dot(out_grad, proj_out, preferred_element_type=jnp.float32)
    in_full, out_full = (
        lax.psum(in_partial.astype(jnp.bfloat16), "mp").astype(jnp.float32),
        lax.psum(out_partial.astype(jnp.bfloat16), "mp").astype(jnp.float32),
    )
    in_weighted = (in_full * tok_scale[:, None]).reshape(doc_count, seq_len, sketch_rank)
    out_three = out_full.reshape(doc_count, seq_len, sketch_rank)
    full_sketch = jnp.einsum(
        "dtr,dts->drs", in_weighted, out_three, precision=lax.Precision.HIGHEST
    )
    full_sketch = full_sketch.reshape(doc_count, sketch_rank * sketch_rank)
    sketch = lax.dynamic_slice_in_dim(full_sketch, lax.axis_index("mp") * feat_count, feat_count, 1)
    stream = pre_norm.astype(jnp.bfloat16)
    sketch_bf = sketch.astype(jnp.bfloat16)
    all_sketch = lax.all_gather(sketch_bf, "dp", axis=0, tiled=True)
    per_query = lax.dot_general(
        all_sketch, queries, (((1,), (1,)), ((), ())), preferred_element_type=jnp.float32
    )
    query_rows = queries.shape[0]
    own_ids = lax.dynamic_slice_in_dim(query_ids, lax.axis_index("dp") * query_rows, query_rows, 0)
    local_scores = jnp.dot(per_query, group_table(own_ids, QG), precision=lax.Precision.HIGHEST)
    summed_scores = lax.psum(local_scores, ("dp", "mp"))
    scores = lax.dynamic_slice_in_dim(summed_scores, lax.axis_index("dp") * doc_count, doc_count, 0)
    return (stream, scores)


def solution(mesh):
    placed = (
        P(("groups", "dp"), None),
        P(("groups", "dp"), "mp"),
        P(("groups", "dp"), "mp"),
        P(("groups", "dp"), "mp"),
        P("mp", None),
        P("mp"),
        P("mp", None),
        P("mp", None),
        P(),
        P(("groups", "dp")),
        P("dp", "mp"),
        P(),
    )
    return jax.shard_map(
        per_device,
        mesh=mesh,
        in_specs=placed,
        out_specs=(P(("groups", "dp"), "mp"), P(("groups", "dp"), None)),
        check_vma=False,
    )
```

profile of v0, /device:TPU:0, one launch (start us, length us, event | category | flops | bytes accessed | tf_op | source)
XLA Modules:
  0.0 495.7 jit_solution(15099142913691858794)
XLA Ops:
  7.2 0.0 copy-start
  7.2 0.0 reduce-scatter.2.cloned.1.call-start
  7.2 96.3 %convolution_convert_fusion = bf16[1024,8192]{1,0:T(8,128)(2,1)} fusion(bf16[1024,5120]{1,0:T(8,128)(2,1)} %param.13, bf16[5120,8192]{1,0:T(8,128)(2,1)} %param.16), kind=kOutput, calls=%fused_computation.1 | convolution fusion | flops 85907734528 | bytes 111149056 | tf_op jit(solution)/shard_map/dot_general | solution.py:44
  103.5 0.0 copy-start.3
  103.5 0.0 copy-start.4
  103.5 0.0 copy-start.2
  103.5 0.0 reduce-scatter.2.cloned.1.call-update
  103.5 0.0 all-reduce.4.cloned.1.call-start
  103.6 0.6 copy-done.3
  104.2 0.0 copy-done.4
  104.2 0.4 copy-done.2
  104.6 7.9 %convolution_convert_fusion.1 = bf16[1024,64]{0,1:T(8,128)(2,1)} fusion(bf16[1024,5120]{1,0:T(8,128)(2,1)} %param.13, bf16[5120,64]{0,1:T(8,128)(2,1)S(1)} %copy-done.2), kind=kOutput, calls=%fused_computation.9 | convolution fusion | flops 671154176 | bytes 11272192 | tf_op jit(solution)/shard_map/dot_general | solution.py:45
  112.5 0.0 copy-start.6
  112.5 274.2 %reduce-scatter.2.cloned.1.call-done = bf16[1024,2048]{1,0:T(8,128)(2,1)} async-done(((bf16[1024,8192]{1,0:T(8,128)(2,1)}), bf16[1024,2048]{1,0:T(8,128)(2,1)}) %reduce-scatter.2.cloned.1.call-update) | async-done | bytes 4194320 | tf_op jit(solution)/shard_map/reduce_scatter | solution.py:51
  386.7 6.8 %multiply_reduce_fusion.1 = (f32[1024]{0:T(1024)S(1)}, f32[1024]{0:T(1024)S(1)}, bf16[1024,2048]{1,0:T(8,128)(2,1)}) fusion(bf16[1024,2048]{1,0:T(8,128)(2,1)} %reduce-scatter.2.cloned.1.call-done, bf16[1024,2048]{1,0:T(8,128)(2,1)} %param.14, bf16[1024,2048]{1,0:T(8,128)(2,1)} %param.15, f32[2048]{0:T(1024)S(1)} %convert_element_type.41), kind=kLoop, calls=%fused_computation.5 | loop fusion | flops 20969472 | bytes 16793600 | tf_op jit(solution)/shard_map/reduce_sum | solution.py:57
  393.5 11.5 %all-reduce = (f32[1024]{0:T(1024)S(1)}, f32[1024]{0:T(1024)S(1)}) all-reduce(f32[1024]{0:T(1024)S(1)} %get-tuple-element.3, f32[1024]{0:T(1024)S(1)} %get-tuple-element.2), channel_id=1, replica_groups=mesh['groups'=2,'dp'=4,'mp'=4] {'mp'}, use_global_device_ids=true, to_apply=%region_5.6 | all-reduce | flops 2048 | bytes 16384 | tf_op jit(solution)/shard_map/psum | solution.py:56
  405.0 0.0 copy-done.6
  405.0 0.0 copy-start.1
  405.0 0.0 copy-start.5
  405.0 6.4 %fusion.2 = bf16[1024,64]{0,1:T(8,128)(2,1)S(1)} fusion(bf16[2048,64]{0,1:T(8,128)(2,1)S(1)} %copy-done.6, bf16[1024,2048]{1,0:T(8,128)(2,1)} %param.15, bf16[1024,2048]{1,0:T(8,128)(2,1)} %reduce-scatter.2.cloned.1.call-done, bf16[1024,2048]{1,0:T(8,128)(2,1)} %param.14, f32[1024]{0:T(1024)S(1)} %get-tuple-element.10, f32[2048]{0:T(1024)S(1)} %convert_element_type.41, ...), kind=kOutput, calls=%fused_computation.10 | convolution fusion | flops 291569664 | bytes 12992512 | tf_op jit(solution)/shard_map/dot_general | solution.py:62
  411.4 0.7 copy.29
  412.1 0.0 all-reduce.4.cloned.1.call-update
  412.1 0.0 copy-done.1
  412.2 6.2 %gather_fusion = f32[1024]{0:T(1024)S(1)} fusion(f32[128256]{0:T(1024)S(1)} %copy-done.1, s32[1024]{0:T(1024)S(1)} %broadcast_clamp_fusion), kind=kCustom, calls=%fused_computation | custom fusion | bytes 12288 | tf_op jit(solution)/shard_map/gather | solution.py:47
  418.3 0.0 copy-done.5
  418.3 0.1 fusion.9
  418.4 0.7 dynamic_slice.10
  419.1 27.1 %all-reduce.4.cloned.1.call-done = (bf16[2,512,64]{1,2,0:T(8,128)(2,1)}, bf16[1024,64]{0,1:T(8,128)(2,1)}) async-done(((bf16[2,512,64]{1,2,0:T(8,128)(2,1)}, bf16[1024,64]{0,1:T(8,128)(2,1)}), (bf16[2,512,64]{1,2,0:T(8,128)(2,1)}, bf16[1024,64]{0,1:T(8,128)(2,1)})) %all-reduce.4.cloned.1.call-update) | async-done | bytes 262160 | tf_op jit(solution)/shard_map/psum | solution.py:65
  446.2 0.9 convert_multiply_fusion.1
  447.1 1.2 fusion.5
  448.3 0.1 reshape.48
  448.4 5.2 %all-gather = bf16[4,2,1024]{2,1,0:T(2,128)(2,1)S(1)} all-gather(bf16[1,2,1024]{2,1,0:T(2,128)(2,1)S(1)} %fusion.10), channel_id=1, replica_groups=mesh['groups'=2,'dp'=4,'mp'=4] {'dp'}, dimensions={0}, use_global_device_ids=true | all-gather | bytes 20480 | tf_op jit(solution)/shard_map/all_gather | solution.py:76
  453.6 0.0 copy-done
  453.6 0.6 fusion.12
  454.2 0.5 fusion.3
  454.7 33.6 %psum.39 = f32[8,256]{1,0:T(8,128)S(1)} all-reduce(f32[8,256]{1,0:T(8,128)S(1)} %fusion.3), channel_id=1, replica_groups=mesh['groups'=2,'dp'=4,'mp'=4] {'dp','mp'}, use_global_device_ids=true, to_apply=%region_7.8 | all-reduce | flops 2048 | bytes 16384 | tf_op jit(solution)/shard_map/psum | solution.py:83
  488.3 0.6 constant_dynamic-slice_fusion
  (9 shorter events, 0.1 us)
Async XLA Ops:
  7.2 446.4 %copy-start = (bf16[1024,1024]{1,0:T(8,128)(2,1)S(1)}, bf16[1024,1024]{1,0:T(8,128)(2,1)}, u32[]{:S(2)}) copy-start(bf16[1024,1024]{1,0:T(8,128)(2,1)} %param.22) | copy-start | bytes 6291460
  7.2 379.5 %reduce-scatter.2.cloned.1.call-start = ((), (), s32[]{:S(2)}) async-start(), calls=%async_computation.1 | async-start | bytes 20971520 | tf_op jit(solution)/shard_map/reduce_scatter | solution.py:51
  103.5 0.7 copy-start.3
  103.5 0.7 copy-start.4
  103.5 1.1 copy-start.2
  103.5 342.6 %all-reduce.4.cloned.1.call-start = ((), (), s32[]{:S(2)}) async-start(), calls=%async_computation.2 | async-start | bytes 524288 | tf_op jit(solution)/shard_map/psum | solution.py:65
  112.5 292.5 %copy-start.6 = (bf16[2048,64]{0,1:T(8,128)(2,1)S(1)}, bf16[2048,64]{0,1:T(8,128)(2,1)}, u32[]{:S(2)}) copy-start(bf16[2048,64]{0,1:T(8,128)(2,1)} %param.19) | copy-start | bytes 786436
  405.0 7.1 %copy-start.1 = (f32[128256]{0:T(1024)S(1)}, f32[128256]{0:T(1024)}, u32[]{:S(2)}) copy-start(f32[128256]{0:T(1024)} %param.20) | copy-start | bytes 1539076
  405.0 13.3 %copy-start.5 = (s32[2]{0:T(128)S(1)}, s32[2]{0:T(128)}, u32[]{:S(2)}) copy-start(s32[2]{0:T(128)} %param.21) | copy-start | bytes 28
Sparse Core Ops, SparseCore 0:
  103.6 283.0 reduce-scatter.1
  412.2 33.8 all-reduce.3
where the time goes:
time: 496 us
  waiting for transfers between devices  301 us (61%)
  matrix products  113 us (23%)
  blocking collectives  50.3 us (10%)
  between operations  14.2 us (3%)
  local copies, waits for them, and re-layouts  9.29 us (2%)
  other arithmetic  7.79 us (2%)
    reduce_scatter x1, waiting for transfers between devices, per_device(): lax.psum_scatter(partial_out.astype(jnp.bfloat16), 'mp', scatter_dimensio...  274 us
    dot_general x1, matrix products, per_device(): partial_out = jnp.dot(acts, weight, preferred_element_type=jnp.float32)  96.3 us
    psum x1, blocking collectives, per_device(): summed_scores = lax.psum(local_scores, ('dp', 'mp'))  33.6 us
    psum x1, waiting for transfers between devices, per_device(): lax.psum(out_partial.astype(jnp.bfloat16), 'mp').astype(jnp.float32)  27.1 us
    psum x1, blocking collectives, per_device(): lax.psum((jnp.sum(pre_norm * pre_norm, axis=1), jnp.sum(pre_norm * scaled...  11.5 us
  transfers between devices with their start and end apart: 2, of which 2 were waited for; matrix products, arithmetic and copies ran while one was open for 3% of the time, Pallas kernels for 0%

commit v1 on v0

v1 whole, which is shorter than its diff:
```python
import jax
import jax.numpy as jnp
from jax import lax
from jax.sharding import PartitionSpec as P

QG = 256
CHUNKS = 4


norm_eps = 1e-05


def split_dot(values, proj):
    high = values.astype(jnp.bfloat16)
    low = (values - high.astype(jnp.float32)).astype(jnp.bfloat16)
    both = jnp.dot(
        jnp.concatenate([high, low], axis=0), proj, preferred_element_type=jnp.float32
    )
    rows = values.shape[0]
    return both[:rows] + both[rows:]


def group_sums(queries, own_ids, group_count):
    table = (jnp.arange(group_count, dtype=jnp.int32)[:, None] == own_ids[None, :]).astype(
        jnp.bfloat16
    )
    return jnp.dot(table, queries, preferred_element_type=jnp.float32)


def score_tail(
    in_and_cot, pre_side, tok_scale, grouped, seq_len, doc_count, sketch_rank, width_full
):
    rows = in_and_cot.shape[0]
    in_sk = in_and_cot[:, :sketch_rank]
    cot_sk = in_and_cot[:, sketch_rank:]
    pre_sk = pre_side[:, :sketch_rank]
    mean_sq = pre_side[:, sketch_rank : sketch_rank + 1] / width_full
    mean_cross = pre_side[:, sketch_rank + 1 : sketch_rank + 2] / width_full
    rstd = lax.rsqrt(mean_sq + norm_eps)
    out_sk = rstd * (cot_sk - pre_sk * (rstd * rstd * mean_cross))
    first = lax.axis_index("mp") * rows
    own_doc = (first + jnp.arange(rows, dtype=jnp.int32)) // seq_len
    own_scale = lax.dynamic_slice_in_dim(tok_scale, first, rows, 0)
    by_doc = jnp.where(
        own_doc[None, :] == jnp.arange(doc_count, dtype=jnp.int32)[:, None],
        own_scale[None, :],
        jnp.float32(0.0),
    )
    weighted = by_doc[:, :, None] * in_sk[None, :, :]
    sketch = jnp.einsum("dtr,ts->drs", weighted, out_sk, precision=lax.Precision.HIGHEST)
    sketch = sketch.reshape(doc_count, sketch_rank * sketch_rank)
    sketch = lax.psum_scatter(sketch, "mp", scatter_dimension=1, tiled=True)
    sketch = sketch.astype(jnp.bfloat16)
    high, low = grouped
    contract = (((1,), (1,)), ((), ()))
    local = lax.dot_general(
        sketch, high, contract, preferred_element_type=jnp.float32
    ) + lax.dot_general(sketch, low, contract, preferred_element_type=jnp.float32)
    return lax.psum(local, "mp")


def per_device(
    tokens,
    acts,
    resid,
    cotangent,
    weight,
    gain,
    proj_in,
    proj_out,
    tok_weight,
    lengths,
    queries,
    query_ids,
):
    doc_count, seq_len = tokens.shape
    tok_count = acts.shape[0]
    sketch_rank = proj_in.shape[1]
    width_full = resid.shape[1] * lax.axis_size("mp")
    rows = tok_count // CHUNKS

    query_rows = queries.shape[0]
    own_ids = lax.dynamic_slice_in_dim(query_ids, lax.axis_index("dp") * query_rows, query_rows, 0)

    alive_mask = jnp.arange(seq_len, dtype=jnp.int32)[None, :] < lengths[:, None]
    tok_scale = jnp.where(alive_mask, tok_weight[tokens], jnp.float32(0.0)) / jnp.sqrt(
        jnp.float32(seq_len)
    )
    tok_scale = tok_scale.reshape(tok_count)

    streams, sides = [], []
    cots = []
    for c in range(CHUNKS):
        part = slice(c * rows, (c + 1) * rows)
        partial = jnp.dot(acts[part], weight, preferred_element_type=jnp.float32)
        layer_out = lax.psum_scatter(
            partial.astype(jnp.bfloat16), "mp", scatter_dimension=1, tiled=True
        ).astype(jnp.float32)
        pre_norm = resid[part].astype(jnp.float32) + layer_out
        scaled_cot = gain.astype(jnp.float32)[None, :] * cotangent[part].astype(jnp.float32)
        cots.append(split_dot(scaled_cot, proj_out))
        sides.append(
            jnp.concatenate(
                [
                    split_dot(pre_norm, proj_out),
                    jnp.sum(pre_norm * pre_norm, axis=1, keepdims=True),
                    jnp.sum(pre_norm * scaled_cot, axis=1, keepdims=True),
                ],
                axis=1,
            )
        )
        streams.append(pre_norm.astype(jnp.bfloat16))
    grouped = lax.psum(group_sums(queries, own_ids, QG), "dp")
    high = grouped.astype(jnp.bfloat16)
    low = (grouped - high.astype(jnp.float32)).astype(jnp.bfloat16)
    in_partial = jnp.dot(acts, proj_in, preferred_element_type=jnp.float32)
    in_and_cot = lax.psum_scatter(
        jnp.concatenate([in_partial, jnp.concatenate(cots, axis=0)], axis=1),
        "mp",
        scatter_dimension=0,
        tiled=True,
    )
    pre_side = lax.psum_scatter(
        jnp.concatenate(sides, axis=0), "mp", scatter_dimension=0, tiled=True
    )
    scores = score_tail(
        in_and_cot,
        pre_side,
        tok_scale,
        (high, low),
        seq_len,
        doc_count,
        sketch_rank,
        width_full,
    )
    return (jnp.concatenate(streams, axis=0), scores)


def solution(mesh):
    placed = (
        P(("groups", "dp"), None),
        P(("groups", "dp"), "mp"),
        P(("groups", "dp"), "mp"),
        P(("groups", "dp"), "mp"),
        P("mp", None),
        P("mp"),
        P("mp", None),
        P("mp", None),
        P(),
        P(("groups", "dp")),
        P("dp", "mp"),
        P(),
    )
    return jax.shard_map(
        per_device,
        mesh=mesh,
        in_specs=placed,
        out_specs=(P(("groups", "dp"), "mp"), P(("groups", "dp"), None)),
        check_vma=False,
    )
```

time: 496 us -> 475 us (0.958)
  matrix products: 113 us -> 153 us
  blocking collectives: 50.3 us -> 10.4 us
  waiting for transfers between devices: 301 us -> 264 us
  other arithmetic: 7.79 us -> 16.5 us
    reduce_scatter x1 -> x6, waiting for transfers between devices: 274 us -> 227 us  [the longest x4 196 us: per_device(): lax.psum_scatter(partial.astype(jnp.bfloat16), 'mp', scatter_dimension=1,...]
    dot_general x5 -> x16, matrix products: 105 us -> 150 us  [the longest x4 138 us: per_device(): partial = jnp.dot(acts[part], weight, preferred_element_type=jnp.float32)]
    unnamed x2 -> x9, waiting for transfers between devices: 0.03 us -> 37 us
    psum x2 -> x1, blocking collectives: 45.1 us -> 10.4 us  [score_tail(): return lax.psum(local, 'mp')]
    psum x1, waiting for transfers between devices: 27.1 us -> 0.01 us  [per_device(): grouped = lax.psum(group_sums(queries, own_ids, QG), 'dp')]
    unnamed x18 -> x36, local copies, waits for them, and re-layouts: 1.09 us -> 6.51 us
    all_gather x1 -> x0, blocking collectives: 5.19 us -> none  [per_device(): all_sketch = lax.all_gather(sketch_bf, 'dp', axis=0, tiled=True)]
    concatenate x0 -> x3, other arithmetic: none -> 5.17 us  [the longest x1 3.58 us: per_device(): return (jnp.concatenate(streams, axis=0), scores)]
  transfers between devices with their start and end apart: 2 -> 8, of which waited for: 2 -> 6; matrix products, arithmetic and copies ran while one was open for 3% -> 29% of each run, Pallas kernels for 0% -> 0%
where the time goes in v1:
time: 475 us; the launch traced here: 474 us
  waiting for transfers between devices  264 us (56%)
  matrix products  153 us (32%)
  other arithmetic  16.5 us (3%)
  between operations  15.9 us (3%)
  local copies, waits for them, and re-layouts  13.6 us (3%)
  blocking collectives  10.4 us (2%)
    reduce_scatter x4, waiting for transfers between devices, per_device(): lax.psum_scatter(partial.astype(jnp.bfloat16), 'mp', scatter_dimension=1,...  196 us
    dot_general x4, matrix products, per_device(): partial = jnp.dot(acts[part], weight, preferred_element_type=jnp.float32)  138 us
    unnamed x9, waiting for transfers between devices  37 us
    reduce_scatter x1, waiting for transfers between devices, per_device(): lax.psum_scatter(jnp.concatenate(sides, axis=0), 'mp', scatter_dimension=...  20.2 us
    reduce_scatter x1, waiting for transfers between devices, per_device(): lax.psum_scatter(jnp.concatenate([in_partial, jnp.concatenate(cots, axis=...  10.8 us
    psum x1, blocking collectives, score_tail(): return lax.psum(local, 'mp')  10.4 us
  transfers between devices with their start and end apart: 8, of which 6 were waited for; matrix products, arithmetic and copies ran while one was open for 29% of the time, Pallas kernels for 0%

profile of v1, /device:TPU:0, one launch (start us, length us, event | category | flops | bytes accessed | tf_op | source)
XLA Modules:
  0.0 474.5 jit_solution(2913549776262684178)
XLA Ops:
  8.0 0.0 copy-start
  8.0 0.0 reduce-scatter.14.cloned.1.call-start
  8.1 33.9 %convolution_convert_fusion.1 = bf16[256,8192]{1,0:T(8,128)(2,1)} fusion(bf16[5120,8192]{1,0:T(8,128)(2,1)} %param.16, bf16[1024,5120]{1,0:T(8,128)(2,1)} %param.13), kind=kOutput, calls=%fused_computation.2 | convolution fusion | flops 21476933632 | bytes 90701824 | tf_op jit(solution)/shard_map/dot_general | solution.py:95
  42.0 0.0 reduce-scatter.14.cloned.1.call-update
  42.0 0.0 reduce-scatter.16.cloned.1.call-start
  42.1 35.0 %convolution_convert_fusion = bf16[256,8192]{1,0:T(8,128)(2,1)} fusion(bf16[5120,8192]{1,0:T(8,128)(2,1)} %param.16, bf16[1024,5120]{1,0:T(8,128)(2,1)} %param.13), kind=kOutput, calls=%fused_computation.1 | convolution fusion | flops 21476933632 | bytes 90701824 | tf_op jit(solution)/shard_map/dot_general | solution.py:95
  77.0 0.0 reduce-scatter.16.cloned.1.call-update
  77.0 0.2 reduce-scatter.10.cloned.1.call-start
  77.3 34.0 %convolution_convert_fusion.3 = bf16[256,8192]{1,0:T(8,128)(2,1)} fusion(bf16[5120,8192]{1,0:T(8,128)(2,1)} %param.16, bf16[1024,5120]{1,0:T(8,128)(2,1)} %param.13), kind=kOutput, calls=%fused_computation.4 | convolution fusion | flops 21476933632 | bytes 90701824 | tf_op jit(solution)/shard_map/dot_general | solution.py:95
  111.3 0.0 reduce-scatter.10.cloned.1.call-update
  111.4 0.0 reduce-scatter.12.cloned.1.call-start
  111.4 34.7 %convolution_convert_fusion.2 = bf16[256,8192]{1,0:T(8,128)(2,1)} fusion(bf16[5120,8192]{1,0:T(8,128)(2,1)} %param.16, bf16[1024,5120]{1,0:T(8,128)(2,1)} %param.13), kind=kOutput, calls=%fused_computation.3 | convolution fusion | flops 21476933632 | bytes 90701824 | tf_op jit(solution)/shard_map/dot_general | solution.py:95
  146.1 0.0 reduce-scatter.12.cloned.1.call-update
  146.1 0.3 reduce-scatter.18.cloned.1.call-start
  146.4 0.4 copy-done.9
  146.8 3.4 fusion.39
  150.2 0.8 fusion.12
  150.9 0.0 slice-start.2
  151.0 0.8 fusion.16
  151.7 0.8 fusion.4
  152.5 0.8 fusion.8
  153.3 0.3 copy-done.8
  153.6 3.3 fusion.77
  156.9 0.8 maximum_maximum_fusion
  157.8 0.0 reduce-scatter.18.cloned.1.call-update
  157.8 0.0 reduce-scatter.20.cloned.1.call-start
  157.9 0.3 copy-done.1
  158.1 6.1 %gather_fusion = f32[1024]{0:T(1024)S(1)} fusion(f32[128256]{0:T(1024)S(1)} %copy-done.1, s32[1024]{0:T(1024)S(1)} %broadcast_clamp_fusion), kind=kCustom, calls=%fused_computation | custom fusion | bytes 12288 | tf_op jit(solution)/shard_map/gather | solution.py:86
  164.3 0.0 reduce-scatter.14.cloned.1.call-done
  164.3 37.0 %reduce-scatter.16.cloned.1.call-done = bf16[256,2048]{1,0:T(8,128)(2,1)} async-done(((bf16[256,8192]{1,0:T(8,128)(2,1)}), bf16[256,2048]{1,0:T(8,128)(2,1)}) %reduce-scatter.16.cloned.1.call-update) | async-done | bytes 1048592 | tf_op jit(solution)/shard_map/reduce_scatter | solution.py:96
  201.3 79.6 %reduce-scatter.10.cloned.1.call-done = bf16[256,2048]{1,0:T(8,128)(2,1)} async-done(((bf16[256,8192]{1,0:T(8,128)(2,1)}), bf16[256,2048]{1,0:T(8,128)(2,1)}) %reduce-scatter.10.cloned.1.call-update) | async-done | bytes 1048592 | tf_op jit(solution)/shard_map/reduce_scatter | solution.py:96
  280.9 79.6 %reduce-scatter.12.cloned.1.call-done = bf16[256,2048]{1,0:T(8,128)(2,1)} async-done(((bf16[256,8192]{1,0:T(8,128)(2,1)}), bf16[256,2048]{1,0:T(8,128)(2,1)}) %reduce-scatter.12.cloned.1.call-update) | async-done | bytes 1048592 | tf_op jit(solution)/shard_map/reduce_scatter | solution.py:96
  360.5 6.2 %multiply_reduce_fusion.6 = (f32[256]{0:T(256)S(1)}, f32[256]{0:T(256)S(1)}, f32[256]{0:T(256)S(1)}, f32[256]{0:T(256)S(1)}, f32[256]{0:T(256)S(1)}, /*index=5*/...) fusion(bf16[256,2048]{1,0:T(8,128)(2,1)} %reduce-scatter.10.clo, ...), kind=kLoop, calls=%fused_computation.51 | loop fusion | flops 27260928 | bytes 18890752 | tf_op jit(solution)/shard_map/reduce_sum | solution.py:107
  366.7 0.8 fusion.20
  367.5 0.8 fusion.24
  368.3 1.5 copy-done.2
  369.8 0.3 copy-done.4
  370.1 0.3 copy-done.5
  370.4 0.8 fusion.42
  371.2 0.8 fusion.28
  372.0 0.2 copy-done.3
  372.2 0.8 fusion.32
  373.0 0.7 maximum_maximum_fusion.1
  373.7 0.0 reduce-scatter.20.cloned.1.call-update
  373.7 0.0 reduce-scatter.22.cloned.1.call-start
  373.8 0.1 fusion.61
  373.9 0.1 dynamic_slice.6
  374.0 10.8 %reduce-scatter.18.cloned.1.call-done = f32[256,128]{0,1:T(8,128)} async-done(((f32[1024,128]{0,1:T(8,128)}), f32[256,128]{0,1:T(8,128)}) %reduce-scatter.18.cloned.1.call-update) | async-done | bytes 131088 | tf_op jit(solution)/shard_map/reduce_scatter | solution.py:117
  384.8 0.8 slice.142
  385.7 20.2 %reduce-scatter.20.cloned.1.call-done = f32[256,66]{0,1:T(8,128)} async-done(((f32[1024,66]{0,1:T(8,128)}), f32[256,66]{0,1:T(8,128)}) %reduce-scatter.20.cloned.1.call-update) | async-done | bytes 67600 | tf_op jit(solution)/shard_map/reduce_scatter | solution.py:123
  405.8 0.8 fusion.65
  406.6 1.1 fusion.49
  407.7 0.0 dynamic-slice-start
  407.8 2.1 copy.16
  409.8 0.0 reduce-scatter.22.cloned.1.call-update
  409.8 0.0 all-reduce.2.cloned.1.call-start
  409.9 1.7 fusion.44
  411.6 0.0 all-reduce.2.cloned.1.call-update
  411.7 3.6 pad_maximum_fusion
  415.2 36.9 %reduce-scatter.22.cloned.1.call-done = f32[1024,2]{1,0:T(8,128)} async-done(((f32[4096,2]{1,0:T(8,128)}), f32[1024,2]{1,0:T(8,128)}) %reduce-scatter.22.cloned.1.call-update) | async-done | bytes 8208
  452.1 1.2 copy.15
  453.3 1.5 fusion.47
  454.8 1.8 convolution_add_fusion
  456.6 10.4 %psum.15 = f32[2,256]{1,0:T(2,128)} all-reduce(f32[2,256]{1,0:T(2,128)S(1)} %convolution_add_fusion), channel_id=1, replica_groups=mesh['groups'=2,'dp'=4,'mp'=4] {'mp'}, use_global_device_ids=true, to_apply=%region_16.17 | all-reduce | flops 512 | bytes 4096 | tf_op jit(solution)/shard_map/psum | solution.py:59
  (38 shorter events, 0.2 us)
Async XLA Ops:
  8.0 401.9 %copy-start = (bf16[1024,1024]{1,0:T(8,128)(2,1)S(1)}, bf16[1024,1024]{1,0:T(8,128)(2,1)}, u32[]{:S(2)}) copy-start(bf16[1024,1024]{1,0:T(8,128)(2,1)} %param.22) | copy-start | bytes 6291460
  8.0 156.3 %reduce-scatter.14.cloned.1.call-start = ((), (), s32[]{:S(2)}) async-start(), calls=%async_computation.9 | async-start | bytes 5242880 | tf_op jit(solution)/shard_map/reduce_scatter | solution.py:96
  42.0 159.3 %reduce-scatter.16.cloned.1.call-start = ((), (), s32[]{:S(2)}) async-start(), calls=%async_computation.10 | async-start | bytes 5242880 | tf_op jit(solution)/shard_map/reduce_scatter | solution.py:96
  77.0 203.9 %reduce-scatter.10.cloned.1.call-start = ((), (), s32[]{:S(2)}) async-start(), calls=%async_computation.7 | async-start | bytes 5242880 | tf_op jit(solution)/shard_map/reduce_scatter | solution.py:96
  111.4 249.1 %reduce-scatter.12.cloned.1.call-start = ((), (), s32[]{:S(2)}) async-start(), calls=%async_computation.8 | async-start | bytes 5242880 | tf_op jit(solution)/shard_map/reduce_scatter | solution.py:96
  146.1 0.7 copy-start.9
  146.1 238.7 %reduce-scatter.18.cloned.1.call-start = ((), (), s32[]{:S(2)}) async-start(), calls=%async_computation.11 | async-start | bytes 655360 | tf_op jit(solution)/shard_map/reduce_scatter | solution.py:117
  146.8 3.4 copy-start.12
  146.8 6.6 %slice-start = ((s8[10485760]{0:T(1024)(128)(4,1)}), s8[4194304]{0:T(1024)(128)(4,1)S(1)}, s32[]{:S(2)}) async-start(s8[10485760]{0:T(1024)(128)(4,1)} %bitcast.40), calls=%async_computation.15 | async-start | bytes 8388608
  146.8 6.6 %slice-start.1 = ((s8[10485760]{0:T(1024)(128)(4,1)}), s8[4194304]{0:T(1024)(128)(4,1)S(1)}, s32[]{:S(2)}) async-start(s8[10485760]{0:T(1024)(128)(4,1)} %bitcast.40), calls=%async_computation.16 | async-start | bytes 8388608
  150.9 2.4 slice-start.2
  152.5 1.1 copy-start.8
  153.6 4.2 copy-start.10
  156.9 1.2 copy-start.1
  157.8 248.0 %reduce-scatter.20.cloned.1.call-start = ((), (), s32[]{:S(2)}) async-start(), calls=%async_computation.12 | async-start | bytes 368640 | tf_op jit(solution)/shard_map/reduce_scatter | solution.py:123
  366.7 1.6 copy-start.6
  366.7 1.6 copy-start.7
  366.7 3.0 copy-start.2
  367.5 2.6 copy-start.4
  367.5 2.9 copy-start.5
  371.2 1.0 copy-start.3
  372.2 1.6 copy-start.11
  373.7 78.4 %reduce-scatter.22.cloned.1.call-start = ((), (), s32[]{:S(2)}) async-start(), calls=%async_computation.14 | async-start | bytes 2621440
  407.7 2.2 dynamic-slice-start
  409.8 43.5 %all-reduce.2.cloned.1.call-start = ((), (), s32[]{:S(2)}) async-start(), calls=%async_computation.13 | async-start | bytes 2097152 | tf_op jit(solution)/shard_map/psum | solution.py:113
Sparse Core Ops, SparseCore 0:
  42.1 79.4 reduce-scatter.13
  124.0 77.2 reduce-scatter.15
  203.6 77.2 reduce-scatter.9
  283.2 77.2 reduce-scatter.11
  362.7 22.0 reduce-scatter.17
  387.6 18.1 reduce-scatter.19
  410.0 42.0 reduce-scatter.21
Sparse Core Ops, SparseCore 1:
  412.7 34.9 all-reduce.1

commit v2 on v0

v2 whole, which is shorter than its diff:
```python
import functools

import jax
import jax.numpy as jnp
from jax import lax
from jax.experimental import pallas as pl
from jax.experimental.pallas import tpu as pltpu
from jax.sharding import PartitionSpec as P

QG = 256
LANES = 128
TILE = 256
ROWS = 256
DOT_ROWS = 512
WSLOTS = 3
MESH = pl.DeviceIdType.MESH


norm_eps = 1e-05


def split(values):
    high = values.astype(jnp.bfloat16)
    return high, (values - high.astype(jnp.float32)).astype(jnp.bfloat16)


def split_dot(values, proj):
    high, low = split(values)
    return jnp.dot(high, proj, preferred_element_type=jnp.float32) + jnp.dot(
        low, proj, preferred_element_type=jnp.float32
    )


def group_sums(queries, own_ids, group_count):
    table = (jnp.arange(group_count, dtype=jnp.int32)[:, None] == own_ids[None, :]).astype(
        jnp.bfloat16
    )
    return jnp.dot(table, queries, preferred_element_type=jnp.float32)


def kernel(
    n,
    rank,
    acts_hbm,
    weight_hbm,
    resid_hbm,
    cot_hbm,
    gain_ref,
    proj_in_ref,
    proj_out_ref,
    scale_ref,
    stream_hbm,
    sketch_ref,
    acts,
    resid,
    cot,
    tiles,
    ring,
    acc,
    cot_side,
    pre_side,
    cot_parts,
    pre_parts,
    sk_own,
    sk_parts,
    load_sems,
    tile_sems,
    ring_send,
    ring_recv,
    out_sems,
    cot_send,
    cot_recv,
    pre_send,
    pre_recv,
    sk_send,
    sk_recv,
):
    me = lax.axis_index("mp")
    right = lax.rem(me + 1, n)
    tok_count = acts.shape[0]
    block = resid.shape[1]
    tile = acc.shape[1]
    subs = block // tile
    total = n * subs
    own_rows = tok_count // n
    width_full = block * n
    row_blk = min(ROWS, tok_count)
    dot_blk = min(DOT_ROWS, tok_count)

    loads = [
        pltpu.make_async_copy(src, dst, load_sems.at[i])
        for i, (src, dst) in enumerate(((acts_hbm, acts), (cot_hbm, cot), (resid_hbm, resid)))
    ]

    def tile_copy(t):
        owner = lax.rem(me - 1 - t // subs + 2 * n, n)
        at = pl.multiple_of(owner * block + lax.rem(t, subs) * tile, tile)
        slot = lax.rem(t, WSLOTS)
        return pltpu.make_async_copy(
            weight_hbm.at[:, pl.ds(at, tile)], tiles.at[slot], tile_sems.at[slot]
        )

    def hop(t):
        return pltpu.make_async_remote_copy(
            src_ref=ring.at[t],
            dst_ref=ring.at[t + subs],
            send_sem=ring_send.at[t],
            recv_sem=ring_recv.at[t + subs],
            device_id={"mp": right},
            device_id_type=MESH,
        )

    def out_copy(j):
        at = pl.multiple_of(j * tile, tile)
        return pltpu.make_async_copy(
            ring.at[total - subs + j], stream_hbm.at[:, pl.ds(at, tile)], out_sems.at[j]
        )

    def spread(source, parts, send, recv, whole):
        copies = []
        for k in range(1, n):
            peer = lax.rem(me + k, n)
            src = source
            if not whole:
                src = source.at[pl.ds(pl.multiple_of(peer * own_rows, own_rows), own_rows)]
            copies.append(
                pltpu.make_async_remote_copy(
                    src_ref=src,
                    dst_ref=parts.at[k - 1],
                    send_sem=send.at[k - 1],
                    recv_sem=recv.at[k - 1],
                    device_id={"mp": peer},
                    device_id_type=MESH,
                )
            )
        return copies

    tile_copy(0).start()
    loads[0].start()
    tile_copy(1).start()
    loads[1].start()
    loads[2].start()

    barrier = pltpu.get_barrier_semaphore()
    for k in range(1, n):
        pl.semaphore_signal(
            barrier, inc=1, device_id={"mp": lax.rem(me + k, n)}, device_id_type=MESH
        )
    pl.semaphore_wait(barrier, n - 1)

    cot_side[...] = jnp.zeros_like(cot_side)
    pre_side[...] = jnp.zeros_like(pre_side)
    loads[0].wait()

    lane = lax.broadcasted_iota(jnp.int32, (row_blk, LANES), 1)

    def scaled(rows, cols):
        return gain_ref[0:1, cols].astype(jnp.float32) * cot[rows, cols].astype(jnp.float32)

    def row_loop(size, body):
        def step(b, carry):
            body(pl.ds(pl.multiple_of(b * size, size), size))
            return carry

        lax.fori_loop(0, tok_count // size, step, 0)

    cot_copies = spread(cot_side, cot_parts, cot_send, cot_recv, False)

    def one(t, carry):
        @pl.when(t + 2 < total)
        def _():
            tile_copy(t + 2).start()

        tile_copy(t).wait()
        slot = lax.rem(t, WSLOTS)

        def mul(rows):
            acc[rows, :] = jnp.dot(
                acts[rows, :], tiles[slot], preferred_element_type=jnp.float32
            )

        row_loop(dot_blk, mul)
        j = lax.rem(t, subs)
        cols = pl.ds(pl.multiple_of(j * tile, tile), tile)

        @pl.when(t < subs)
        def _():
            def put(rows):
                ring[t, rows, :] = acc[rows, :].astype(jnp.bfloat16)

            row_loop(row_blk, put)
            hop(t).start()

            @pl.when(t == 0)
            def _():
                loads[1].wait()
                loads[2].wait()

            def side(rows):
                cot_side[rows, :] += split_dot(scaled(rows, cols), proj_out_ref[cols, :])

            row_loop(row_blk, side)

            @pl.when(t == subs - 1)
            def _():
                def ins(rows):
                    cot_side[rows, :] += jnp.dot(
                        acts[rows, :], proj_in_ref[...], preferred_element_type=jnp.float32
                    )

                row_loop(row_blk, ins)
                for copy in cot_copies:
                    copy.start()

        @pl.when(t >= subs)
        def _():
            hop(t - subs).wait_recv()

        @pl.when(jnp.logical_and(t >= subs, t < total - subs))
        def _():
            def add(rows):
                ring[t, rows, :] = (acc[rows, :] + ring[t, rows, :].astype(jnp.float32)).astype(
                    jnp.bfloat16
                )

            row_loop(row_blk, add)
            hop(t).start()

        @pl.when(t >= total - subs)
        def _():
            def last(rows):
                pre = resid[rows, cols].astype(jnp.float32) + (
                    acc[rows, :] + ring[t, rows, :].astype(jnp.float32)
                )
                ring[t, rows, :] = pre.astype(jnp.bfloat16)
                squares = jnp.sum(pre * pre, axis=1, keepdims=True)
                crosses = jnp.sum(pre * scaled(rows, cols), axis=1, keepdims=True)
                extra = jnp.where(
                    lane == rank, squares, jnp.where(lane == rank + 1, crosses, jnp.float32(0.0))
                )
                pre_side[rows, :] += split_dot(pre, proj_out_ref[cols, :]) + extra

            row_loop(row_blk, last)
            out_copy(j).start()

        return carry

    lax.fori_loop(0, total, one, 0)

    pre_copies = spread(pre_side, pre_parts, pre_send, pre_recv, False)
    for copy in pre_copies:
        copy.start()
    mine = pl.ds(pl.multiple_of(me * own_rows, own_rows), own_rows)
    cots = cot_side[mine, :]
    for k in range(1, n):
        cot_copies[k - 1].wait_recv()
        cots += cot_parts[k - 1]
    pres = pre_side[mine, :]
    for k in range(1, n):
        pre_copies[k - 1].wait_recv()
        pres += pre_parts[k - 1]
    rstd = lax.rsqrt(pres[:, rank : rank + 1] / width_full + norm_eps)
    factor = rstd * rstd * (pres[:, rank + 1 : rank + 2] / width_full)
    own_lane = lax.broadcasted_iota(jnp.int32, (own_rows, LANES), 1)
    outs = jnp.where(own_lane < rank, rstd * (cots - pres * factor), jnp.float32(0.0))
    for d in range(scale_ref.shape[1]):
        full = lax.dot_general(
            cots,
            outs * scale_ref[:, d : d + 1],
            (((0,), (0,)), ((), ())),
            preferred_element_type=jnp.float32,
            precision=lax.Precision.HIGHEST,
        )
        sk_own[d] = full[LANES - rank :, :]
    sk_copies = spread(sk_own, sk_parts, sk_send, sk_recv, True)
    for copy in sk_copies:
        copy.start()
    sums = sk_own[...]
    for k in range(1, n):
        sk_copies[k - 1].wait_recv()
        sums += sk_parts[k - 1]
    sketch_ref[...] = sums

    def drain(t, carry):
        hop(t).wait_send()
        return carry

    lax.fori_loop(0, total - subs, drain, 0)

    def drain_out(j, carry):
        out_copy(j).wait()
        return carry

    lax.fori_loop(0, subs, drain_out, 0)
    for copy in cot_copies + pre_copies + sk_copies:
        copy.wait_send()


def per_device(
    tokens,
    acts,
    resid,
    cotangent,
    weight,
    gain,
    proj_in,
    proj_out,
    tok_weight,
    lengths,
    queries,
    query_ids,
):
    doc_count, seq_len = tokens.shape
    tok_count, depth = acts.shape
    rank = proj_in.shape[1]
    block = resid.shape[1]
    feat_count = queries.shape[1]
    n = lax.axis_size("mp")
    me = lax.axis_index("mp")
    tile = min(TILE, block)
    subs = block // tile
    own_rows = tok_count // n

    query_rows = queries.shape[0]
    own_ids = lax.dynamic_slice_in_dim(query_ids, lax.axis_index("dp") * query_rows, query_rows, 0)
    grouped = lax.psum(group_sums(queries, own_ids, QG), "dp")

    place = me * own_rows + jnp.arange(own_rows, dtype=jnp.int32)
    own_tokens = lax.dynamic_slice_in_dim(tokens.reshape(tok_count), me * own_rows, own_rows, 0)
    docs = jnp.arange(doc_count, dtype=jnp.int32)[None, :]
    alive = jnp.logical_and(
        (place // seq_len)[:, None] == docs, (place % seq_len)[:, None] < lengths[None, :]
    )
    scale = jnp.where(alive, tok_weight[own_tokens][:, None], jnp.float32(0.0)) / jnp.sqrt(
        jnp.float32(seq_len)
    )

    bf16, f32 = jnp.bfloat16, jnp.float32
    any_space = pl.BlockSpec(memory_space=pl.ANY)
    vmem = pl.BlockSpec(memory_space=pltpu.VMEM)
    dma = pltpu.SemaphoreType.DMA
    stream, sketch = pl.pallas_call(
        functools.partial(kernel, n, rank),
        out_shape=(
            jax.ShapeDtypeStruct((tok_count, block), bf16),
            jax.ShapeDtypeStruct((doc_count, rank, LANES), f32),
        ),
        in_specs=[any_space] * 4 + [vmem] * 4,
        out_specs=(any_space, vmem),
        scratch_shapes=[
            pltpu.VMEM((tok_count, depth), bf16),
            pltpu.VMEM((tok_count, block), bf16),
            pltpu.VMEM((tok_count, block), bf16),
            pltpu.VMEM((WSLOTS, depth, tile), bf16),
            pltpu.VMEM((n * subs, tok_count, tile), bf16),
            pltpu.VMEM((tok_count, tile), f32),
            pltpu.VMEM((tok_count, LANES), f32),
            pltpu.VMEM((tok_count, LANES), f32),
            pltpu.VMEM((n - 1, own_rows, LANES), f32),
            pltpu.VMEM((n - 1, own_rows, LANES), f32),
            pltpu.VMEM((doc_count, rank, LANES), f32),
            pltpu.VMEM((n - 1, doc_count, rank, LANES), f32),
            dma((3,)),
            dma((WSLOTS,)),
            dma((n * subs,)),
            dma((n * subs,)),
            dma((subs,)),
        ]
        + [dma((n - 1,))] * 6,
        compiler_params=pltpu.CompilerParams(
            collective_id=0, has_side_effects=True, vmem_limit_bytes=60 * 1024 * 1024
        ),
        cost_estimate=pl.CostEstimate(
            flops=2 * tok_count * depth * block * n,
            bytes_accessed=2 * depth * block * n,
            transcendentals=0,
        ),
    )(
        acts,
        weight,
        resid,
        cotangent,
        gain.reshape(1, block),
        jnp.pad(proj_in, ((0, 0), (LANES - rank, 0))),
        jnp.pad(proj_out, ((0, 0), (0, LANES - rank))),
        scale,
    )

    sketch = sketch[:, :, :rank].reshape(doc_count, rank * rank).astype(bf16)
    sketch = lax.dynamic_slice_in_dim(sketch, me * feat_count, feat_count, 1)
    high, low = split(grouped)
    contract = (((1,), (1,)), ((), ()))
    local = lax.dot_general(
        sketch, high, contract, preferred_element_type=f32
    ) + lax.dot_general(sketch, low, contract, preferred_element_type=f32)
    return (stream, lax.psum(local, "mp"))


def solution(mesh):
    placed = (
        P(("groups", "dp"), None),
        P(("groups", "dp"), "mp"),
        P(("groups", "dp"), "mp"),
        P(("groups", "dp"), "mp"),
        P("mp", None),
        P("mp"),
        P("mp", None),
        P("mp", None),
        P(),
        P(("groups", "dp")),
        P("dp", "mp"),
        P(),
    )
    return jax.shard_map(
        per_device,
        mesh=mesh,
        in_specs=placed,
        out_specs=(P(("groups", "dp"), "mp"), P(("groups", "dp"), None)),
        check_vma=False,
    )
```

time: 496 us -> 365 us (0.74)
  Pallas kernels: 0 us -> 313 us
  waiting for transfers between devices: 301 us -> 0.03 us
  matrix products: 113 us -> 4.99 us
  blocking collectives: 50.3 us -> 14 us
  local copies, waits for them, and re-layouts: 9.29 us -> 17.3 us
  other arithmetic: 7.79 us -> 0.93 us
    pallas_call x0 -> x1, Pallas kernels: none -> 313 us  [per_device(): pl.pallas_call(functools.partial(kernel, n, rank), out_shape=(jax.ShapeDt...]
    reduce_scatter x1 -> x0, waiting for transfers between devices: 274 us -> none  [per_device(): lax.psum_scatter(partial_out.astype(jnp.bfloat16), 'mp', scatter_dimensio...]
    dot_general x6 -> x3, matrix products: 113 us -> 4.99 us  [the longest x1 1.81 us: per_device(): lax.dot_general(sketch, low, contract, preferred_element_type=f32)]
    psum x2 -> x1, blocking collectives: 45.1 us -> 14 us  [per_device(): return (stream, lax.psum(local, 'mp'))]
    psum x1, waiting for transfers between devices: 27.1 us -> 0.02 us  [per_device(): grouped = lax.psum(group_sums(queries, own_ids, QG), 'dp')]
    unnamed x18 -> x12, local copies, waits for them, and re-layouts: 1.09 us -> 9.12 us
    reduce_sum x1 -> x0, other arithmetic: 6.77 us -> none  [per_device(): jnp.sum(pre_norm * pre_norm, axis=1)]
    all_gather x1 -> x0, blocking collectives: 5.19 us -> none  [per_device(): all_sketch = lax.all_gather(sketch_bf, 'dp', axis=0, tiled=True)]
  transfers between devices with their start and end apart: 2 -> 1, of which waited for: 2 -> 0; matrix products, arithmetic and copies ran while one was open for 3% -> 3% of each run, Pallas kernels for 0% -> 86%
where the time goes in v2:
time: 365 us
  Pallas kernels  313 us (86%)
  local copies, waits for them, and re-layouts  17.3 us (5%)
  between operations  14.1 us (4%)
  blocking collectives  14 us (4%)
  matrix products  4.99 us (1%)
    pallas_call x1, Pallas kernels, per_device(): pl.pallas_call(functools.partial(kernel, n, rank), out_shape=(jax.ShapeDt...  313 us
    psum x1, blocking collectives, per_device(): return (stream, lax.psum(local, 'mp'))  14 us
    unnamed x12, local copies, waits for them, and re-layouts  9.12 us
  transfers between devices with their start and end apart: 1, of which 0 were waited for; matrix products, arithmetic and copies ran while one was open for 3% of the time, Pallas kernels for 86%

profile of v2, /device:TPU:0, one launch (start us, length us, event | category | flops | bytes accessed | tf_op | source)
XLA Modules:
  0.0 364.8 jit_solution(1991236856171368449)
XLA Ops:
  7.2 0.0 copy-start
  7.2 0.0 copy-start.2
  7.2 0.0 all-reduce.4.cloned.1.call-start
  7.2 0.8 dynamic_slice.11
  8.1 0.7 copy-done
  8.8 1.7 fusion
  10.5 0.0 copy-start.1
  10.5 0.0 copy-start.3
  10.5 0.0 all-reduce.4.cloned.1.call-update
  10.5 0.0 copy-done.2
  10.6 0.1 compare_select_fusion
  10.6 1.7 copy.16
  12.3 2.0 copy.17
  14.3 1.5 pad.8.proj_in_ref
  15.8 1.9 pad.9.proj_out_ref
  17.7 0.0 copy-done.1
  17.7 0.6 reshape.47.gain_ref
  18.3 2.3 gather_fusion
  20.6 0.0 copy-done.3
  20.6 0.8 select_multiply_fusion.scale_ref
  21.5 313.4 %shard_map.131 = (bf16[1024,2048]{1,0:T(8,128)(2,1)}, f32[2,64,128]{2,1,0:T(8,128)}) custom-call(bf16[1024,5120]{1,0:T(8,128)(2,1)} %acts_hbm.1, bf16[5120,8192]{1,0:T(8,128)(2,1)} %weight_hbm.1, bf16[1024,2048]{1,0:T(8,128)(2,1)} %resid_hbm.1, bf16[1024,2048]{1,0:T(8,128)(2,1)} %cot_hbm.1, bf16[1,2048]{1,0:T(2,128)(2,1)} %reshape.47.gain_ref, ...), custom_call_target="tpu_custom_call" | custom-call | flops 85899345920 | bytes 83886080 | tf_op jit(solution)/shard_map/pallas_call | solution.py:342
  334.8 0.8 slice.9
  335.7 0.1 convert_element_type.18
  335.8 0.0 all-reduce.4.cloned.1.call-done
  335.8 1.5 fusion.3
  337.3 1.8 convolution_add_fusion
  339.1 14.0 %psum.15 = f32[2,256]{1,0:T(2,128)} all-reduce(f32[2,256]{1,0:T(2,128)S(1)} %convolution_add_fusion), channel_id=1, replica_groups=mesh['groups'=2,'dp'=4,'mp'=4] {'mp'}, use_global_device_ids=true, to_apply=%region_1.2 | all-reduce | flops 512 | bytes 4096 | tf_op jit(solution)/shard_map/psum | solution.py:396
  353.1 4.8 %copy.21 = bf16[1024,2048]{1,0:T(8,128)(2,1)} copy(bf16[1024,2048]{1,0:T(8,128)(2,1)} %get-tuple-element.10) | data formatting | bytes 8388608
  (3 shorter events, 0.0 us)
Async XLA Ops:
  7.2 1.6 copy-start
  7.2 3.4 copy-start.2
  7.2 328.6 %all-reduce.4.cloned.1.call-start = ((), (), s32[]{:S(2)}) async-start(), calls=%async_computation | async-start | bytes 2097152 | tf_op jit(solution)/shard_map/psum | solution.py:326
  10.5 7.2 %copy-start.1 = (bf16[2048]{0:T(1024)(128)(2,1)S(1)}, bf16[2048]{0:T(1024)(128)(2,1)}, u32[]{:S(2)}) copy-start(bf16[2048]{0:T(1024)(128)(2,1)} %param.17) | copy-start | bytes 12292
  10.5 10.1 %copy-start.3 = (s32[2]{0:T(128)S(1)}, s32[2]{0:T(128)}, u32[]{:S(2)}) copy-start(s32[2]{0:T(128)} %param.21) | copy-start | bytes 28
Sparse Core Ops, SparseCore 0:
  10.6 38.8 all-reduce.3

commit v3 on v2

--- a/solution.py
+++ b/solution.py
@@ -24,11 +24,15 @@
     return high, (values - high.astype(jnp.float32)).astype(jnp.bfloat16)
 
 
+def dot_t(left, right):
+    return lax.dot_general(
+        left, right, (((1,), (1,)), ((), ())), preferred_element_type=jnp.float32
+    )
+
+
 def split_dot(values, proj):
     high, low = split(values)
-    return jnp.dot(high, proj, preferred_element_type=jnp.float32) + jnp.dot(
-        low, proj, preferred_element_type=jnp.float32
-    )
+    return dot_t(high, proj) + dot_t(low, proj)
 
 
 def group_sums(queries, own_ids, group_count):
@@ -59,8 +63,13 @@
     acc,
     cot_side,
     pre_side,
-    cot_parts,
-    pre_parts,
+    wide_in,
+    wide_out,
+    stats,
+    stat_parts,
+    flat,
+    both,
+    both_parts,
     sk_own,
     sk_parts,
     load_sems,
@@ -68,10 +77,10 @@
     ring_send,
     ring_recv,
     out_sems,
-    cot_send,
-    cot_recv,
-    pre_send,
-    pre_recv,
+    stat_send,
+    stat_recv,
+    both_send,
+    both_recv,
     sk_send,
     sk_recv,
 ):
@@ -150,6 +159,10 @@
 
     cot_side[...] = jnp.zeros_like(cot_side)
     pre_side[...] = jnp.zeros_like(pre_side)
+    wide_in[...] = jnp.zeros_like(wide_in)
+    wide_in[LANES - rank :, :] = proj_in_ref[...]
+    wide_out[...] = jnp.zeros_like(wide_out)
+    wide_out[:rank, :] = proj_out_ref[...]
     loads[0].wait()
 
     lane = lax.broadcasted_iota(jnp.int32, (row_blk, LANES), 1)
@@ -164,8 +177,6 @@
 
         lax.fori_loop(0, tok_count // size, step, 0)
 
-    cot_copies = spread(cot_side, cot_parts, cot_send, cot_recv, False)
-
     def one(t, carry):
         @pl.when(t + 2 < total)
         def _():
@@ -197,20 +208,16 @@
                 loads[2].wait()
 
             def side(rows):
-                cot_side[rows, :] += split_dot(scaled(rows, cols), proj_out_ref[cols, :])
+                cot_side[rows, :] += split_dot(scaled(rows, cols), wide_out[:, cols])
 
             row_loop(row_blk, side)
 
             @pl.when(t == subs - 1)
             def _():
                 def ins(rows):
-                    cot_side[rows, :] += jnp.dot(
-                        acts[rows, :], proj_in_ref[...], preferred_element_type=jnp.float32
-                    )
+                    cot_side[rows, :] += dot_t(acts[rows, :], wide_in[...])
 
                 row_loop(row_blk, ins)
-                for copy in cot_copies:
-                    copy.start()
 
         @pl.when(t >= subs)
         def _():
@@ -238,7 +245,7 @@
                 extra = jnp.where(
                     lane == rank, squares, jnp.where(lane == rank + 1, crosses, jnp.float32(0.0))
                 )
-                pre_side[rows, :] += split_dot(pre, proj_out_ref[cols, :]) + extra
+                pre_side[rows, :] += split_dot(pre, wide_out[:, cols]) + extra
 
             row_loop(row_blk, last)
             out_copy(j).start()
@@ -247,25 +254,37 @@
 
     lax.fori_loop(0, total, one, 0)
 
-    pre_copies = spread(pre_side, pre_parts, pre_send, pre_recv, False)
-    for copy in pre_copies:
+    stats[...] = pre_side[...].T[rank : rank + 8, :]
+    stat_copies = spread(stats, stat_parts, stat_send, stat_recv, True)
+    for copy in stat_copies:
+        copy.start()
+    flat[...] = jnp.zeros_like(flat)
+    sums = stats[...]
+    for k in range(1, n):
+        stat_copies[k - 1].wait_recv()
+        sums += stat_parts[k - 1]
+    flat[0:8, :] = sums
+    pre_stats = flat[...].T
+    rstd = lax.rsqrt(pre_stats[:, 0:1] / width_full + norm_eps)
+    factor = rstd * rstd * (pre_stats[:, 1:2] / width_full)
+    cots = cot_side[...]
+    all_lane = lax.broadcasted_iota(jnp.int32, (tok_count, LANES), 1)
+    both[...] = jnp.where(
+        all_lane < rank, rstd * (cots - pre_side[...] * factor), cots
+    ).astype(jnp.bfloat16)
+    both_copies = spread(both, both_parts, both_send, both_recv, False)
+    for copy in both_copies:
         copy.start()
     mine = pl.ds(pl.multiple_of(me * own_rows, own_rows), own_rows)
-    cots = cot_side[mine, :]
-    for k in range(1, n):
-        cot_copies[k - 1].wait_recv()
-        cots += cot_parts[k - 1]
-    pres = pre_side[mine, :]
-    for k in range(1, n):
-        pre_copies[k - 1].wait_recv()
-        pres += pre_parts[k - 1]
-    rstd = lax.rsqrt(pres[:, rank : rank + 1] / width_full + norm_eps)
-    factor = rstd * rstd * (pres[:, rank + 1 : rank + 2] / width_full)
+    sides = both[mine, :].astype(jnp.float32)
+    for k in range(1, n):
+        both_copies[k - 1].wait_recv()
+        sides += both_parts[k - 1].astype(jnp.float32)
     own_lane = lax.broadcasted_iota(jnp.int32, (own_rows, LANES), 1)
-    outs = jnp.where(own_lane < rank, rstd * (cots - pres * factor), jnp.float32(0.0))
+    outs = jnp.where(own_lane < rank, sides, jnp.float32(0.0))
     for d in range(scale_ref.shape[1]):
         full = lax.dot_general(
-            cots,
+            sides,
             outs * scale_ref[:, d : d + 1],
             (((0,), (0,)), ((), ())),
             preferred_element_type=jnp.float32,
@@ -292,7 +311,38 @@
         return carry
 
     lax.fori_loop(0, subs, drain_out, 0)
-    for copy in cot_copies + pre_copies + sk_copies:
+    for copy in stat_copies + both_copies + sk_copies:
+        copy.wait_send()
+
+
+def score_kernel(n, sketch_ref, high_ref, low_ref, out_ref, own, parts, send, recv):
+    me = lax.axis_index("mp")
+    barrier = pltpu.get_barrier_semaphore()
+    for k in range(1, n):
+        pl.semaphore_signal(
+            barrier, inc=1, device_id={"mp": lax.rem(me + k, n)}, device_id_type=MESH
+        )
+    own[...] = dot_t(sketch_ref[...], high_ref[...]) + dot_t(sketch_ref[...], low_ref[...])
+    pl.semaphore_wait(barrier, n - 1)
+    copies = [
+        pltpu.make_async_remote_copy(
+            src_ref=own,
+            dst_ref=parts.at[k - 1],
+            send_sem=send.at[k - 1],
+            recv_sem=recv.at[k - 1],
+            device_id={"mp": lax.rem(me + k, n)},
+            device_id_type=MESH,
+        )
+        for k in range(1, n)
+    ]
+    for copy in copies:
+        copy.start()
+    sums = own[...]
+    for k in range(1, n):
+        copies[k - 1].wait_recv()
+        sums += parts[k - 1]
+    out_ref[...] = sums
+    for copy in copies:
         copy.wait_send()
 
 
@@ -356,8 +406,13 @@
             pltpu.VMEM((tok_count, tile), f32),
             pltpu.VMEM((tok_count, LANES), f32),
             pltpu.VMEM((tok_count, LANES), f32),
-            pltpu.VMEM((n - 1, own_rows, LANES), f32),
-            pltpu.VMEM((n - 1, own_rows, LANES), f32),
+            pltpu.VMEM((LANES, depth), bf16),
+            pltpu.VMEM((LANES, block), bf16),
+            pltpu.VMEM((8, tok_count), f32),
+            pltpu.VMEM((n - 1, 8, tok_count), f32),
+            pltpu.VMEM((LANES, tok_count), f32),
+            pltpu.VMEM((tok_count, LANES), bf16),
+            pltpu.VMEM((n - 1, own_rows, LANES), bf16),
             pltpu.VMEM((doc_count, rank, LANES), f32),
             pltpu.VMEM((n - 1, doc_count, rank, LANES), f32),
             dma((3,)),
@@ -381,19 +436,30 @@
         resid,
         cotangent,
         gain.reshape(1, block),
-        jnp.pad(proj_in, ((0, 0), (LANES - rank, 0))),
-        jnp.pad(proj_out, ((0, 0), (0, LANES - rank))),
+        proj_in.T,
+        proj_out.T,
         scale,
     )
 
     sketch = sketch[:, :, :rank].reshape(doc_count, rank * rank).astype(bf16)
     sketch = lax.dynamic_slice_in_dim(sketch, me * feat_count, feat_count, 1)
     high, low = split(grouped)
-    contract = (((1,), (1,)), ((), ()))
-    local = lax.dot_general(
-        sketch, high, contract, preferred_element_type=f32
-    ) + lax.dot_general(sketch, low, contract, preferred_element_type=f32)
-    return (stream, lax.psum(local, "mp"))
+    scores = pl.pallas_call(
+        functools.partial(score_kernel, n),
+        out_shape=jax.ShapeDtypeStruct((doc_count, QG), f32),
+        in_specs=[vmem] * 3,
+        out_specs=vmem,
+        scratch_shapes=[
+            pltpu.VMEM((doc_count, QG), f32),
+            pltpu.VMEM((n - 1, doc_count, QG), f32),
+            dma((n - 1,)),
+            dma((n - 1,)),
+        ],
+        compiler_params=pltpu.CompilerParams(
+            collective_id=1, has_side_effects=True, vmem_limit_bytes=16 * 1024 * 1024
+        ),
+    )(sketch, high, low)
+    return (stream, scores)
 
 
 def solution(mesh):

time: 365 us -> 339 us (0.929)
  blocking collectives: 14 us -> 0 us
  local copies, waits for them, and re-layouts: 17.3 us -> 10.2 us
  Pallas kernels: 313 us -> 309 us
    psum x1 -> x0, blocking collectives: 14 us -> none  [per_device(): return (stream, lax.psum(local, 'mp'))]
    pallas_call x1, Pallas kernels: 313 us -> 304 us  [per_device(): pl.pallas_call(functools.partial(kernel, n, rank), out_shape=(jax.ShapeDt...]
    pallas_call x0 -> x1, Pallas kernels: none -> 5.96 us  [per_device(): pl.pallas_call(functools.partial(score_kernel, n), out_shape=jax.ShapeDty...]
    unnamed x12 -> x13, local copies, waits for them, and re-layouts: 9.12 us -> 6.06 us
  transfers between devices with their start and end apart: 1 -> 1, of which waited for: 0 -> 0; matrix products, arithmetic and copies ran while one was open for 3% -> 1% of each run, Pallas kernels for 86% -> 90%
where the time goes in v3:
time: 339 us; the launch traced here: 338 us
  Pallas kernels  309 us (91%)
  between operations  14.2 us (4%)
  local copies, waits for them, and re-layouts  10.2 us (3%)
    pallas_call x1, Pallas kernels, per_device(): pl.pallas_call(functools.partial(kernel, n, rank), out_shape=(jax.ShapeDt...  304 us
  transfers between devices with their start and end apart: 1, of which 0 were waited for; matrix products, arithmetic and copies ran while one was open for 1% of the time, Pallas kernels for 90%

profile of v3, /device:TPU:0, one launch (start us, length us, event | category | flops | bytes accessed | tf_op | source)
XLA Modules:
  0.0 338.3 jit_solution(17924939354979993337)
XLA Ops:
  7.2 0.0 copy-start
  7.2 0.0 copy-start.3
  7.2 0.0 copy-start.2
  7.2 0.0 copy-start.1
  7.2 0.0 copy-start.4
  7.2 0.0 all-reduce.2.cloned.1.call-start
  7.3 0.8 dynamic_slice.11
  8.1 0.7 copy-done
  8.8 1.7 fusion
  10.5 0.0 all-reduce.2.cloned.1.call-update
  10.5 0.0 copy-done.3
  10.5 0.1 compare_select_fusion
  10.6 0.0 copy-done.2
  10.6 0.6 reshape.47.gain_ref
  11.2 0.0 copy-done.1
  11.2 1.7 gather_fusion
  13.0 0.0 copy-done.4
  13.0 0.8 select_multiply_fusion.scale_ref
  13.8 303.5 %shard_map.131 = (bf16[1024,2048]{1,0:T(8,128)(2,1)}, f32[2,64,128]{2,1,0:T(8,128)}) custom-call(bf16[1024,5120]{1,0:T(8,128)(2,1)} %acts_hbm.1, bf16[5120,8192]{1,0:T(8,128)(2,1)} %weight_hbm.1, bf16[1024,2048]{1,0:T(8,128)(2,1)} %resid_hbm.1, bf16[1024,2048]{1,0:T(8,128)(2,1)} %cot_hbm.1, bf16[1,2048]{1,0:T(2,128)(2,1)} %reshape.47.gain_ref, ...), custom_call_target="tpu_custom_call" | custom-call | flops 85899345920 | bytes 83886080 | tf_op jit(solution)/shard_map/pallas_call | solution.py:392
  317.3 0.8 slice.9
  318.2 0.1 convert_element_type.14
  318.3 0.0 all-reduce.2.cloned.1.call-done
  318.3 1.8 subtract_convert_fusion
  320.1 6.0 %shard_map.132 = f32[2,256]{1,0:T(2,128)S(1)} custom-call(bf16[2,1024]{1,0:T(2,128)(2,1)S(1)} %constant_dynamic-slice_fusion.sketch_ref, bf16[256,1024]{1,0:T(8,128)(2,1)S(1)} %get-tuple-element.7.high_ref, bf16[256,1024]{1,0:T(8,128)(2,1)S(1)} %get-tuple-element.6.low_ref), custom_call_target="tpu_custom_call" | custom-call | tf_op jit(solution)/shard_map/pallas_call | solution.py:447
  326.1 4.8 %copy.18 = bf16[1024,2048]{1,0:T(8,128)(2,1)} copy(bf16[1024,2048]{1,0:T(8,128)(2,1)} %get-tuple-element.12) | data formatting | bytes 8388608
  330.9 0.6 copy.19
  (4 shorter events, 0.0 us)
Async XLA Ops:
  7.2 1.6 copy-start
  7.2 3.3 copy-start.3
  7.2 3.4 %copy-start.2 = (bf16[2048]{0:T(1024)(128)(2,1)S(1)}, bf16[2048]{0:T(1024)(128)(2,1)}, u32[]{:S(2)}) copy-start(bf16[2048]{0:T(1024)(128)(2,1)} %param.17) | copy-start | bytes 12292
  7.2 4.0 %copy-start.1 = (f32[128256]{0:T(1024)S(1)}, f32[128256]{0:T(1024)}, u32[]{:S(2)}) copy-start(f32[128256]{0:T(1024)} %param.20) | copy-start | bytes 1539076
  7.2 5.8 %copy-start.4 = (s32[2]{0:T(128)S(1)}, s32[2]{0:T(128)}, u32[]{:S(2)}) copy-start(s32[2]{0:T(128)} %param.21) | copy-start | bytes 28
  7.2 311.1 %all-reduce.2.cloned.1.call-start = ((), (), s32[]{:S(2)}) async-start(), calls=%async_computation | async-start | bytes 2097152 | tf_op jit(solution)/shard_map/psum | solution.py:376
Sparse Core Ops, SparseCore 0:
  11.0 38.8 all-reduce.1
